TPU v7x, 128 devices: a whole 4x4x4 slice. The times are simulated.
128 devices in a mesh: seq: 8 (over x_lo, z), clip: 16 (over y, x_hi, core).
Axes of the slice: x: 4 (x_hi: 2, x_lo: 2; x = x_hi * 2 + x_lo), y: 4, z: 4, core: 2. Of those that a mesh axis runs over, the one named last changes fastest.
Arguments:
- clip_features: bfloat16 [16, 4, 16, 64, 384], P('clip', None, 'seq'), may hold values from -6 to 6
- enc_weight: bfloat16 [3, 3, 3, 384, 16], replicated, may hold values from -0.0625 to 0.0625
- noise_field: float32 [16, 4, 16, 64, 16], P('clip', None, 'seq'), may hold values from -6 to 6
- flow_times: int32 [16, 2], P('clip'), may hold values from 0 to 1000, as said below
- embed_weight: bfloat16 [64, 5120], replicated, may hold values from -0.75 to 0.75
- time_weight: bfloat16 [256, 5120], replicated, may hold values from -0.375 to 0.375
- norm_gain: float32 [5120], replicated, may hold values from 0.25 to 1.75
- qkv_weight: bfloat16 [5120, 3, 3072], P('clip', None, 'seq'), may hold values from -0.078125 to 0.078125
Outputs:
- attn_out: bfloat16 [16, 1024, 3072], P('clip', 'seq')
- attn_tangent: bfloat16 [16, 1024, 3072], P('clip', 'seq')
Inputs may be any that keep to these rules, and one draw needn't show every extreme that they name: flow_times[c] = (index of r, index of t) with the index of r at most that of t; some clip has r index 0 and some t index 1000.
All inputs are finite; a program needn't handle non-finite values.
Results may differ from a plain program's by a relative error of at most 0.0044.
Values may be sent and summed in bfloat16 or wider, within the bound.
No kernel may reach another device: no remote copies, remote signals or barrier semaphores. Data moves between devices by JAX's collectives and lax.ppermute only.
A program may use at most 128 MiB of HBM per device.

v0:
```python
import jax
import jax.numpy as jnp
import numpy as np
from jax import lax
from jax.experimental import pallas as pl
from jax.experimental.pallas import tpu as pltpu
from jax.sharding import PartitionSpec as P

D = 5120
HD = 128
TFEAT = 256
TGRID = 1000
EPSILON = 1e-06
QUARTER = TFEAT // 4
F32 = jnp.float32
BF = jnp.bfloat16
HIGH = lax.Precision.HIGHEST
LOG2E = 1.4426950408889634
LN2 = 0.6931471805599453
VMEM = pl.BlockSpec(memory_space=pltpu.VMEM)
SMEM = pl.BlockSpec(memory_space=pltpu.SMEM)
ANY = pl.BlockSpec(memory_space=pl.ANY)
HBM = pl.BlockSpec(memory_space=pltpu.HBM)


def whole(shape):
    return pl.BlockSpec(shape, lambda i: (0,) * len(shape))


def params(limit=63):
    return pltpu.CompilerParams(vmem_limit_bytes=limit * 1024 * 1024)


def dot(a, b, dims=((1,), (0,)), precision=None):
    return lax.dot_general(a, b, (dims, ((), ())), preferred_element_type=F32, precision=precision)


def split(x):
    hi = x.astype(BF)
    return hi, (x - hi.astype(F32)).astype(BF)


def iota(shape, axis):
    return lax.broadcasted_iota(jnp.int32, shape, axis)


def fold_kernel(flow_ref, embed_ref, gain_ref, weight_ref, out_ref, e_ref, g_ref, w_ref, sems):
    rows = out_ref.shape[0]
    _, depth, width = weight_ref.shape
    window = e_ref.shape[1]
    at_clip = lax.axis_index("clip")
    odd = at_clip % 2
    base = pl.multiple_of(at_clip * depth - odd * 64, 128)
    copies = [
        pltpu.make_async_copy(embed_ref.at[:, pl.ds(base, window)], e_ref, sems.at[0]),
        pltpu.make_async_copy(gain_ref.at[:, pl.ds(base, window)], g_ref, sems.at[1]),
    ] + [pltpu.make_async_copy(weight_ref.at[i], w_ref.at[i], sems.at[2 + i]) for i in range(3)]
    for copy in copies:
        copy.start()
    lane = iota((rows, 128), 1)
    start, finish = flow_ref[0, 0], flow_ref[0, 1]
    coded = jnp.where(
        lane == 0,
        start // 256,
        jnp.where(lane == 1, start % 256, jnp.where(lane == 2, finish // 256, finish % 256)),
    )
    row, col = iota((rows, 64), 0), iota((rows, 64), 1)
    twice = jnp.where(col == (row // 8) * 4 + row % 4, 1.0, 0.0).astype(BF)
    copies[0].wait()
    copies[1].wait()
    scaled = dot(twice, e_ref[...]) * g_ref[...]
    scaled = jnp.where(odd == 1, scaled[:, 64 : 64 + depth], scaled[:, :depth])
    scaled_hi, scaled_lo = split(scaled)
    first = (iota((rows, 1), 0) // 4) % 2 == 0
    totals = []
    for i in range(3):
        copies[2 + i].wait()
        totals.append(dot(scaled_hi, w_ref[i]) + dot(scaled_lo, w_ref[i]))
    total = jnp.concatenate(totals + [coded.astype(F32)], axis=1)
    half = out_ref.shape[1]
    out_ref[...] = jnp.where(first, total[:, :half], total[:, half:]).astype(BF)


def frequencies():
    k = iota((1, 128), 1) % QUARTER
    return 8.0 * jnp.exp(k.astype(F32) * np.float32(-np.log(100.0) / QUARTER))


def time_kernel(got_ref, time_ref, gain_ref, weight_ref, out_ref, r_ref, t_ref, g_ref, w_ref, sems):
    rows = out_ref.shape[0]
    groups = rows // 8
    _, depth, width = weight_ref.shape
    window = t_ref.shape[1]
    at_clip = lax.axis_index("clip")
    odd = at_clip % 2
    base = pl.multiple_of(at_clip * depth - odd * 64, 128)
    copies = [
        pltpu.make_async_copy(got_ref, r_ref, sems.at[0]),
        pltpu.make_async_copy(gain_ref.at[:, pl.ds(base, window)], g_ref, sems.at[1]),
        pltpu.make_async_copy(time_ref.at[:, pl.ds(base, window)], t_ref, sems.at[2]),
    ] + [pltpu.make_async_copy(weight_ref.at[i], w_ref.at[i], sems.at[3 + i]) for i in range(3)]
    for copy in copies:
        copy.start()
    freqs = frequencies()
    half_width = r_ref.shape[1]
    copies[0].wait()
    codes = r_ref[:, 3 * width - half_width :].astype(F32)
    start = (codes[:, 0:1] * 256.0 + codes[:, 1:2]) / TGRID
    finish = (codes[:, 2:3] * 256.0 + codes[:, 3:4]) / TGRID
    half = iota((rows, 128), 1) < QUARTER
    angle = freqs * jnp.where(half, finish, finish - start)
    sines, cosines = jnp.sin(angle), jnp.cos(angle)
    place = iota((rows, 1), 0) % 8
    is_value = (place == 4) | (place == 5)
    is_tangent = place >= 6
    first = jnp.where(is_value, sines, jnp.where(is_tangent, freqs * cosines, 0.0))
    second = jnp.where(is_value, cosines, jnp.where(is_tangent, -freqs * sines, 0.0))
    first_hi, first_lo = split(first)
    second_hi, second_lo = split(second)
    copies[1].wait()
    copies[2].wait()
    q = QUARTER
    t_first = jnp.concatenate([t_ref[0:q], t_ref[2 * q : 3 * q]], axis=0)
    t_second = jnp.concatenate([t_ref[q : 2 * q], t_ref[3 * q : 4 * q]], axis=0)
    tau = dot(first_hi, t_first) + dot(first_lo, t_first) + dot(second_hi, t_second) + dot(second_lo, t_second)
    tau = tau * g_ref[...]
    tau = jnp.where(odd == 1, tau[:, 64 : 64 + depth], tau[:, :depth])
    tau_hi, tau_lo = split(tau)
    keep_hi = place % 2 == 0
    summed = r_ref[...].astype(F32).reshape(groups, 8, half_width).sum(axis=0)
    turned = jnp.concatenate([summed[4:], summed[:4]], axis=0)
    summed = jnp.concatenate([summed, turned], axis=1)
    for i in range(3):
        cols = slice(i * width, (i + 1) * width)
        copies[3 + i].wait()
        w = w_ref[i]
        part = dot(tau_hi, w) + dot(tau_lo, w)
        hi = part.astype(BF).astype(F32)
        part = jnp.where(keep_hi, hi, part - hi)
        mine = jnp.concatenate([summed[:, cols]] * groups, axis=0)
        out_ref[:, cols] = jnp.where(place < 4, mine, part).astype(BF)


def head_rows_kernel(got_ref, conv_ref, out_ref):
    rows = got_ref.shape[0]
    heads = 3
    row, col = iota((128, rows), 0), iota((128, rows), 1)
    patch = (row < 64) & (col == (row // 4) * 8 + row % 4)
    place = col % 8
    value = (row >= 64) & (row < 68) & ((place == 4) | (place == 5))
    tangent = (row >= 68) & (row < 72) & (place >= 6)
    pick = jnp.where(patch | value | tangent, 1.0, 0.0).astype(BF)
    total = dot(pick, got_ref[...])
    width = total.shape[1] // 3
    low_row = lambda r: (r == 67) | (r == 71)
    r, l = iota((80, HD), 0), iota((80, HD), 1)
    products, values = [], []
    for h in range(heads):
        part = lambda i: total[:, i * width + h * HD : i * width + (h + 1) * HD]
        q_hi, q_lo = split(part(0)[:80])
        k_hi, k_lo = split(part(1))
        nt = ((1,), (1,))
        product = dot(q_hi, k_hi, nt) + dot(q_lo, k_hi, nt) + dot(q_hi, k_lo, nt)
        hi = product.astype(BF).astype(F32)
        lo = product - hi
        product = jnp.where(low_row(l), jnp.where(r < 64, lo, 0.0), jnp.where(low_row(r), lo, hi))
        products.append(product)
        v = part(2)[:80]
        v_hi = v.astype(BF).astype(F32)
        values.append(jnp.where(low_row(r), v - v_hi, v_hi))
    one, two, three = products
    first = jnp.where(l < 64, one, pltpu.roll(two, 64, 1))
    second = jnp.where(
        l < 64,
        three,
        jnp.where(
            l < 72,
            one,
            jnp.where(l < 80, pltpu.roll(two, 8, 1), jnp.where(l < 88, pltpu.roll(three, 16, 1), 0.0)),
        ),
    )
    blocks = [first, second] + values
    times = jnp.concatenate([b[64:72] for b in blocks] + [jnp.zeros((8, HD), F32)], axis=0).astype(BF)
    for i in range(out_ref.shape[0]):
        for b, block in enumerate(blocks):
            out_ref[i, b * 64 : (b + 1) * 64, :] = block[:64].astype(BF)
        out_ref[i, 320:368, :] = times
        out_ref[i, 368:560, :] = conv_ref[...]


def conv_kernel(x_hbm, w_hbm, noise_hbm, after_ref, out_ref, xp_ref, wt_ref, x_ref, w_ref, noise_ref, sems):
    copies = [
        pltpu.make_async_copy(x_hbm, x_ref, sems.at[0]),
        pltpu.make_async_copy(w_hbm, w_ref, sems.at[1]),
        pltpu.make_async_copy(noise_hbm, noise_ref, sems.at[2]),
    ]
    for copy in copies:
        copy.start()
    for copy in copies:
        copy.wait()
    chans = x_ref.shape[2]
    row, col = iota((128, 128), 0), iota((128, 128), 1)
    row_w = 2 * (row % 32) + (row // 32) % 2
    same = (row // 64) == (col // 64)
    for e in range(3):
        perm = jnp.where(same & (col % 64 == row_w + (e - 1)), 1.0, 0.0).astype(BF)
        for f in range(4):
            moved = dot(perm, x_ref[f]).astype(BF)
            for g in range(4):
                xp_ref[g * 128 + f * 32 : g * 128 + f * 32 + 32, e * chans : (e + 1) * chans] = moved[
                    g * 32 : g * 32 + 32
                ]
        for ab in range(9):
            tap = (ab * 3 + e) * 16
            wt_ref[ab * 16 : ab * 16 + 16, e * chans : (e + 1) * chans] = w_ref[tap : tap + 16, :]
    y = dot(wt_ref[...], xp_ref[...], ((1,), (1,)))
    lane = iota((16, 128), 1)

    def part(a, b, p, q):
        at = (a * 3 + b) * 16
        g = p * 2 + q
        return y[at : at + 16, g * 128 : (g + 1) * 128]

    def frames(of):
        one = jnp.where(lane >= 32, pltpu.roll(of(1), 32, 1), 0.0)
        two = jnp.where(lane >= 64, pltpu.roll(of(0), 64, 1), 0.0)
        return of(2) + one + two

    for q in range(2):
        own0 = frames(lambda a: part(a, 1, 0, q) + part(a, 2, 1, q))
        own1 = frames(lambda a: part(a, 0, 0, q) + part(a, 1, 1, q))
        down = frames(lambda a: part(a, 0, 1, q))
        up = frames(lambda a: part(a, 2, 0, q))
        out_ref[q * 16 : q * 16 + 16, :] = own0.astype(BF)
        out_ref[32 + q * 16 : 48 + q * 16, :] = own1.astype(BF)
        out_ref[128 + q * 16 : 144 + q * 16, :] = down.astype(BF)
        out_ref[160 + q * 16 : 176 + q * 16, :] = up.astype(BF)
    r2, c2 = iota((256, 256), 0), iota((256, 256), 1)
    spread = ((r2 // 64) == (c2 // 32) % 4) & (r2 % 64 == 2 * (c2 % 32) + c2 // 128)
    spread = jnp.where(spread, 1.0, 0.0)
    noise = jnp.concatenate(
        [jnp.concatenate([noise_ref[f, p] for f in range(4)], axis=1) for p in range(2)], axis=0
    )
    moved = dot(noise, spread, precision=HIGH)
    for p in range(2):
        for q in range(2):
            at = 64 + (p * 2 + q) * 16
            out_ref[at : at + 16, :] = moved[p * 16 : p * 16 + 16, q * 128 : (q + 1) * 128].astype(BF)


def gram_kernel(flow_ref, embed_hbm, time_hbm, after_ref, out_ref, embed_ref, time_ref, sems):
    copies = [
        pltpu.make_async_copy(time_hbm, time_ref, sems.at[0]),
        pltpu.make_async_copy(embed_hbm, embed_ref, sems.at[1]),
    ]
    for copy in copies:
        copy.start()
    start = flow_ref[0, 0].astype(F32) / TGRID
    finish = flow_ref[0, 1].astype(F32) / TGRID
    freqs = frequencies()
    angle = freqs * jnp.where(iota((8, 128), 1) < QUARTER, finish, finish - start)
    sines, cosines = jnp.sin(angle), jnp.cos(angle)
    row = iota((8, 128), 0)
    first = jnp.where(row == 0, sines, jnp.where(row == 1, freqs * cosines, 0.0))
    second = jnp.where(row == 0, cosines, jnp.where(row == 1, -freqs * sines, 0.0))
    q = QUARTER
    feats = jnp.concatenate([first[:, :q], second[:, :q], first[:, q:], second[:, q:]], axis=1)
    feat_hi, feat_lo = split(feats)
    feat_mid = (feats - feat_hi.astype(F32) - feat_lo.astype(F32)).astype(BF)
    feats = jnp.concatenate([feat_hi, feat_lo, feat_mid, jnp.zeros_like(feat_hi)], axis=0)
    for copy in copies:
        copy.wait()
    tau = dot(feats, time_ref[...])
    tau = tau[0:8] + tau[8:16] + tau[16:24]
    embed = embed_ref[...]
    out_ref[0:64, 0:64] = dot(embed, embed, ((1,), (1,)))
    tau_hi, tau_lo = split(tau)
    tau_mid = (tau - tau_hi.astype(F32) - tau_lo.astype(F32)).astype(BF)
    taus = jnp.concatenate([tau_hi, tau_lo, tau_mid, jnp.zeros_like(tau_hi)], axis=0)
    cross = dot(embed, taus, ((1,), (1,)))
    out_ref[0:64, 64:128] = jnp.concatenate(
        [cross[:, 0:8] + cross[:, 8:16] + cross[:, 16:24], jnp.zeros((64, 56), F32)], axis=1
    )
    out_ref[64:72, :] = jnp.sum(tau * tau[0:1], axis=1, keepdims=True) + jnp.zeros((8, 128), F32)


def time_coefs(s_hi, s_lo, c_hi, c_lo, kind):
    r = iota((8, s_hi.shape[1]), 0)

    def coefs(high, low):
        if kind == 0:
            return jnp.where((r % 4 == 0) | (r % 4 == 3), high, jnp.where(r % 4 == 1, low, 0.0))
        return jnp.where(r % 4 == 2, low, high)

    plain = jnp.where(r < 4, coefs(s_hi, s_lo), 0.0)
    tangent = jnp.where(r < 4, coefs(c_hi, c_lo), coefs(s_hi, s_lo))
    return plain, tangent


def attention_kernel(flow_ref, n_ref, gram_ref, out_ref, dout_ref, keep_ref, aq_ref, as_ref, ad_ref, av_ref, *scratch):
    peers = n_ref.shape[0]
    tokens = peers * 128
    heads = 3
    rows = heads * 128
    chunk = 16
    zero = lambda r, c=HD: jnp.zeros((r, c), BF)
    cat = lambda xs, axis=0: jnp.concatenate(xs, axis=axis)
    up = lambda x: x.astype(BF).astype(F32)

    flow_t = flow_ref[0, 1].astype(F32) / TGRID
    patches, tangents = [], []
    none = jnp.zeros((32, 128), F32)
    for i in range(peers):
        above = n_ref[i - 1, 496:528].astype(F32) if i > 0 else none
        below = n_ref[i + 1, 528:560].astype(F32) if i + 1 < peers else none
        latent = n_ref[i, 368:432].astype(F32) + cat([above, below])
        noise = n_ref[i, 432:496].astype(F32)
        patches.append((1.0 - flow_t) * latent + flow_t * noise)
        tangents.append(noise - latent)
    p, dp = cat(patches, 1), cat(tangents, 1)
    gp = dot(gram_ref[0:64, 0:64], p, precision=HIGH)
    e_tau, e_dtau = gram_ref[0:64, 64:65], gram_ref[0:64, 65:66]
    mean_sq = jnp.sum(p * (gp + 2.0 * e_tau), axis=0, keepdims=True) + gram_ref[64:65, 0:1]
    mean_sq = jnp.maximum(mean_sq * (1.0 / D), 0.0)
    mixed = jnp.sum(gp * dp + p * e_dtau + dp * e_tau, axis=0, keepdims=True) + gram_ref[65:66, 0:1]
    s = lax.rsqrt(mean_sq + EPSILON)
    c = -(s * s * s) * (mixed * (1.0 / D))
    a = p * s
    da = dp * s + p * c
    a_hi, da_hi = up(a), up(da)
    s_hi, c_hi = up(s), up(c)
    coefs = (s_hi, s - s_hi, c_hi, c - c_hi)
    m_s, m_d = time_coefs(*coefs, 1)
    v_s, v_d = time_coefs(*coefs, 0)
    gap = lambda n: jnp.zeros((n, tokens), F32)
    as_ref[...] = cat([a_hi, a_hi, a - a_hi, m_s, gap(56)]).astype(BF)
    ad_ref[...] = cat([a_hi, da_hi, a_hi, m_s, gap(8), m_d, gap(40)]).astype(BF)
    av_ref[...] = cat([a_hi, a_hi, da_hi, v_s, v_d, v_s, v_d, gap(32)]).T.astype(BF)
    keep_ref[...] = cat([a, da, v_s, v_d])
    own = pl.multiple_of(lax.axis_index("seq") * 128, 128)
    mine = keep_ref[:, pl.ds(own, 128)]
    a, da = mine[0:64], mine[64:128]
    a_hi, da_hi = up(a), up(da)
    gap = jnp.zeros((120, 128), F32)
    aq_ref[0:128, :] = cat([a_hi, a - a_hi, mine[128:136], gap]).T.astype(BF)
    aq_ref[128:256, :] = cat([da_hi, da - da_hi, mine[136:144], gap]).T.astype(BF)

    lane = iota((128, 256), 1)
    low_s = ((lane >= 64) & (lane < 128)) | (lane == 193) | (lane == 197)
    low_d = ((lane >= 128) & (lane < 192)) | (lane == 193) | (lane == 209) | (lane == 213)
    from_q = ((lane >= 64) & (lane < 128)) | (lane >= 200)
    lane = iota((256, 256), 1)
    low_r = ((lane >= 64) & (lane < 128)) | (lane >= 208)
    l = iota((72, HD), 1)

    def times(g, block):
        return n_ref[g, 320:368].astype(F32)[8 * block : 8 * block + 8]

    def scores(g):
        s_ref, d_ref = scratch[4 * (g % 2) : 4 * (g % 2) + 2]
        made = {}

        def absorb(h):
            first = cat([n_ref[g, 0:64].astype(F32), times(g, 0)])
            second = cat([n_ref[g, 64:128].astype(F32), times(g, 1)])
            block = (first, pltpu.roll(first, 64, 1), second)[h]
            swapped = (pltpu.roll(first, 64, 1), first, pltpu.roll(second, 64, 1))[h]
            early = pltpu.roll(second, HD - 8 * h, 1) if h else second
            late = pltpu.roll(second, 16 - 8 * h, 1) if h < 2 else second
            again = jnp.where(
                l < 64, block, jnp.where(l < 72, early, jnp.where((l >= 80) & (l < 88), late, 0.0))
            )
            b = cat([jnp.where(l < 64, block, swapped), again], 1)
            b = cat([b, jnp.zeros((8, 256), F32)]).astype(BF)
            b = cat([b[:64], b[:64], b[64:], zero(112, 256)])
            absorbed = dot(aq_ref[...], b) * (LOG2E * HD ** -0.5)
            hi = absorbed.astype(BF).astype(F32)
            lo = absorbed - hi
            x = jnp.where(low_s, lo[:128], hi[:128]).astype(BF)
            low = jnp.where(from_q, lo[:128], lo[128:])
            high = jnp.where(from_q, hi[:128], hi[128:])
            made[h] = (x, jnp.where(low_d, low, high).astype(BF))

        def score(j, which):
            cols = slice(j * 256, (j + 1) * 256)
            x = cat([made[h][which] for h in range(heads)])
            if which == 0:
                s_ref[:, cols] = dot(x, as_ref[:, cols])
            else:
                d_ref[:, cols] = dot(x, ad_ref[:, cols])

        parts = [lambda h=h: absorb(h) for h in range(heads)]
        tiles = as_ref.shape[1] // 256
        return parts + [lambda j=j, w=w: score(j, w) for w in (0, 1) for j in range(tiles)]

    def softmax(g):
        s_ref, d_ref, et_ref, l_ref = scratch[4 * (g % 2) : 4 * (g % 2) + 4]

        def step(i):
            r = slice(i * chunk, (i + 1) * chunk)
            s = s_ref[r]
            e = jnp.exp2(s - jnp.max(s, axis=1, keepdims=True))
            d = d_ref[r]
            inv = 1.0 / jnp.sum(e, axis=1, keepdims=True)
            mean = jnp.sum(e * d, axis=1, keepdims=True) * inv
            et_ref[r] = e.astype(BF)
            et_ref[rows + i * chunk : rows + (i + 1) * chunk] = (e * (d - mean)).astype(BF)
            l_ref[r] = jnp.broadcast_to(inv, (chunk, 128))

        return [lambda i=i: step(i) for i in range(rows // chunk)]

    def outputs(g):
        et_ref, l_ref = scratch[4 * (g % 2) + 2 : 4 * (g % 2) + 4]
        made = {}

        def mixing():
            made[0] = cat([dot(et_ref[k * 128 : (k + 1) * 128], av_ref[...]) for k in range(2 * heads)])

        def output(h):
            mixes = made[0]
            at = 128 + h * 64
            mv = n_ref[g, at : at + 64]
            t = times(g, 2 + h)
            blank = jnp.zeros((8, HD), F32)
            early, late = cat([t, blank]).astype(BF), cat([blank, t]).astype(BF)
            inv = l_ref[h * 128 : (h + 1) * 128, 0:1]
            mix = mixes[h * 128 : (h + 1) * 128] * inv
            mix_t = mixes[rows + h * 128 : rows + (h + 1) * 128] * (inv * LN2)
            nx = cat([mv, mv, zero(64), early, early, zero(32)])
            ny = cat([zero(128), mv, late, late, zero(32)])
            both = cat([mix, mix_t])
            hi = both.astype(BF).astype(F32)
            both = jnp.where(low_r, both - hi, hi).astype(BF)
            z = dot(both, cat([nx, ny], 1))
            cols = slice((g * heads + h) * HD, (g * heads + h + 1) * HD)
            out_ref[:, cols] = z[:128, :HD].astype(BF)
            dout_ref[:, cols] = (z[128:, :HD] + z[:128, HD:]).astype(BF)

        return [mixing] + [lambda h=h: output(h) for h in range(heads)]

    for part in scores(0):
        part()
    for g in range(peers):
        matmuls = (outputs(g - 1) if g > 0 else []) + (scores(g + 1) if g + 1 < peers else [])
        steps = softmax(g)
        done = 0
        for i, step in enumerate(steps):
            while done < len(matmuls) and done * len(steps) <= i * len(matmuls):
                matmuls[done]()
                done += 1
            step()
        for part in matmuls[done:]:
            part()
    for part in outputs(peers - 1):
        part()


def local(clip_features, enc_weight, noise_field, flow_times, embed_weight, time_weight, norm_gain, qkv_weight):
    clips = lax.axis_size("clip")
    peers = lax.axis_size("seq")
    depth = qkv_weight.shape[0]
    width = qkv_weight.shape[2]
    weight = qkv_weight.transpose(1, 0, 2)
    gain = norm_gain[None]
    shape = jax.ShapeDtypeStruct
    rows = 8 * clips
    heads = width // HD
    tokens = 128 * peers
    window = depth + 64
    half = (3 * width + 128) // 2

    partial = pl.pallas_call(
        fold_kernel,
        grid=(1,),
        out_shape=shape((rows, half), BF),
        in_specs=[SMEM, HBM, HBM, HBM],
        out_specs=whole((rows, half)),
        scratch_shapes=[
            pltpu.VMEM((64, window), BF),
            pltpu.VMEM((1, window), F32),
            pltpu.VMEM((3, depth, width), BF),
            pltpu.SemaphoreType.DMA((5,)),
        ],
        compiler_params=params(),
        name="fold",
    )(flow_times, embed_weight, gain, weight)
    got = lax.all_to_all(partial.reshape(clips, 8, -1), "clip", 0, 0, tiled=True).reshape(rows, -1)

    conv = pl.pallas_call(
        conv_kernel,
        grid=(1,),
        out_shape=shape((192, 128), BF),
        in_specs=[HBM, HBM, HBM, ANY],
        out_specs=whole((192, 128)),
        scratch_shapes=[
            pltpu.VMEM((512, 3 * 384), BF),
            pltpu.VMEM((144, 3 * 384), BF),
            pltpu.VMEM((4, 128, 384), BF),
            pltpu.VMEM((432, 384), BF),
            pltpu.VMEM((4, 2, 16, 64), F32),
            pltpu.SemaphoreType.DMA((3,)),
        ],
        compiler_params=params(),
        name="conv",
    )(
        clip_features.reshape(4, 128, 384),
        enc_weight.transpose(0, 1, 2, 4, 3).reshape(432, 384),
        noise_field[0].transpose(0, 1, 3, 2),
        partial,
    )
    got, conv = lax.optimization_barrier((got, conv))

    second = pl.pallas_call(
        time_kernel,
        grid=(1,),
        out_shape=shape((rows, 3 * width), BF),
        in_specs=[ANY, HBM, HBM, HBM],
        out_specs=whole((rows, 3 * width)),
        scratch_shapes=[
            pltpu.VMEM((rows, half), BF),
            pltpu.VMEM((TFEAT, window), BF),
            pltpu.VMEM((1, window), F32),
            pltpu.VMEM((3, depth, width), BF),
            pltpu.SemaphoreType.DMA((6,)),
        ],
        compiler_params=params(62),
        name="time_rows",
    )(got, time_weight, gain, weight)
    got = lax.all_to_all(second.reshape(clips, 8, -1), "clip", 0, 0, tiled=True).reshape(rows, -1)

    gram = pl.pallas_call(
        gram_kernel,
        grid=(1,),
        out_shape=shape((72, 128), F32),
        in_specs=[SMEM, HBM, HBM, ANY],
        out_specs=whole((72, 128)),
        scratch_shapes=[
            pltpu.VMEM(embed_weight.shape, BF),
            pltpu.VMEM(time_weight.shape, BF),
            pltpu.SemaphoreType.DMA((2,)),
        ],
        compiler_params=params(),
        name="gram",
    )(flow_times, embed_weight, time_weight, second)
    got, gram = lax.optimization_barrier((got, gram))

    folded = pl.pallas_call(
        head_rows_kernel,
        grid=(1,),
        out_shape=shape((peers, 560, 128), BF),
        in_specs=[whole((rows, 3 * width)), whole((192, 128))],
        out_specs=whole((peers, 560, 128)),
        compiler_params=params(24),
        name="head_rows",
    )(got, conv)
    every = lax.all_to_all(folded, "seq", 0, 0, tiled=True)

    out, dout = pl.pallas_call(
        attention_kernel,
        grid=(1,),
        out_shape=[shape((128, peers * width), BF)] * 2,
        in_specs=[SMEM, whole((peers, 560, 128)), whole((72, 128))],
        out_specs=[whole((128, peers * width))] * 2,
        scratch_shapes=[pltpu.VMEM((144, tokens), F32), pltpu.VMEM((256, 256), BF)]
        + [pltpu.VMEM((256, tokens), BF)] * 2
        + [pltpu.VMEM((tokens, 256), BF)]
        + [
            pltpu.VMEM((heads * 128, tokens), F32),
            pltpu.VMEM((heads * 128, tokens), F32),
            pltpu.VMEM((2 * heads * 128, tokens), BF),
            pltpu.VMEM((heads * 128, 128), F32),
        ]
        * 2,
        compiler_params=params(),
        name="attention",
    )(flow_times, every, gram)
    return (out[None], dout[None])


def solution(mesh):
    placed = (
        P("clip", None, "seq", None, None),
        P(),
        P("clip", None, "seq", None, None),
        P("clip", None),
        P(),
        P(),
        P(),
        P("clip", None, "seq"),
    )
    return jax.shard_map(
        local,
        mesh=mesh,
        in_specs=placed,
        out_specs=(P("clip", "seq", None), P("clip", "seq", None)),
        check_vma=False,
    )
```

profile of v0, /device:TPU:0, one launch (start us, length us, event | category | flops | bytes accessed | tf_op | source)
XLA Modules:
  0.0 73.7 jit_solution(12456729029672112650)
XLA Ops:
  0.6 3.4 %fold.1.after_ref = bf16[128,640]{1,0:T(8,128)(2,1)} custom-call(s32[1,2]{1,0:T(1,128)} %flow_ref.5, bf16[64,5120]{1,0:T(8,128)(2,1)} %embed_hbm.1, f32[1,5120]{1,0:T(1,128)} %bitcast.23, bf16[3,320,384]{2,1,0:T(8,128)(2,1)} %bitcast.16), custom_call_target="tpu_custom_call" | custom-call | tf_op jit(solution)/shard_map/fold/pallas_call | solution.py:472
  4.0 7.1 %all-to-all-start = ((bf16[16,8,640]{2,1,0:T(8,128)(2,1)}), bf16[16,8,640]{2,1,0:T(8,128)(2,1)S(1)}, u32[]{:S(2)}, u32[]{:S(2)}) async-start(bf16[16,8,640]{2,1,0:T(8,128)(2,1)} %bitcast.19), calls=%async_computation | async-start | bytes 327680 | tf_op jit(solution)/shard_map/all_to_all | solution.py:487
  11.2 2.8 %conv.1.conv_ref = bf16[192,128]{1,0:T(8,128)(2,1)} custom-call(bf16[4,128,384]{2,1,0:T(8,128)(2,1)} %bitcast.21, bf16[432,384]{1,0:T(8,128)(2,1)} %bitcast.22, f32[4,2,16,64]{3,2,1,0:T(8,128)} %bitcast.25, bf16[128,640]{1,0:T(8,128)(2,1)} %fold.1.after_ref), custom_call_target="tpu_custom_call" | custom-call | tf_op jit(solution)/shard_map/conv/pallas_call | solution.py:489
  14.0 5.8 %all-to-all-done = bf16[16,8,640]{2,1,0:T(8,128)(2,1)S(1)} async-done(((bf16[16,8,640]{2,1,0:T(8,128)(2,1)}), bf16[16,8,640]{2,1,0:T(8,128)(2,1)S(1)}, u32[]{:S(2)}, u32[]{:S(2)}) %all-to-all-start) | async-done | bytes 163872 | tf_op jit(solution)/shard_map/all_to_all | solution.py:487
  19.8 0.0 copy-start.1
  19.8 0.7 copy-done.1
  20.4 3.6 %time_rows.1.after_ref = bf16[128,1152]{1,0:T(8,128)(2,1)} custom-call(bf16[128,640]{1,0:T(8,128)(2,1)} %bitcast.20, bf16[256,5120]{1,0:T(8,128)(2,1)} %time_hbm.1, f32[1,5120]{1,0:T(1,128)} %bitcast.24, bf16[3,320,384]{2,1,0:T(8,128)(2,1)} %bitcast.17), custom_call_target="tpu_custom_call" | custom-call | tf_op jit(solution)/shard_map/time_rows/pallas_call | solution.py:513
  24.0 3.5 %all-to-all-start.1 = ((bf16[16,8,1152]{2,1,0:T(8,128)(2,1)}), bf16[16,8,1152]{2,1,0:T(8,128)(2,1)S(1)}, u32[]{:S(2)}, u32[]{:S(2)}) async-start(bf16[16,8,1152]{2,1,0:T(8,128)(2,1)} %bitcast.18), calls=%async_computation.1 | async-start | bytes 589824 | tf_op jit(solution)/shard_map/all_to_all | solution.py:529
  27.6 0.0 copy-start
  27.6 4.4 %gram.1.gram_ref = f32[72,128]{1,0:T(8,128)} custom-call(s32[1,2]{1,0:T(1,128)} %flow_ref.5, bf16[64,5120]{1,0:T(8,128)(2,1)} %embed_hbm.1, bf16[256,5120]{1,0:T(8,128)(2,1)} %time_hbm.1, bf16[128,1152]{1,0:T(8,128)(2,1)} %time_rows.1.after_ref), custom_call_target="tpu_custom_call" | custom-call | tf_op jit(solution)/shard_map/gram/pallas_call | solution.py:531
  32.0 5.5 %all-to-all-done.1 = bf16[16,8,1152]{2,1,0:T(8,128)(2,1)S(1)} async-done(((bf16[16,8,1152]{2,1,0:T(8,128)(2,1)}), bf16[16,8,1152]{2,1,0:T(8,128)(2,1)S(1)}, u32[]{:S(2)}, u32[]{:S(2)}) %all-to-all-start.1) | async-done | bytes 294944 | tf_op jit(solution)/shard_map/all_to_all | solution.py:529
  37.4 0.0 copy-done
  37.4 0.6 head_rows.1
  38.1 21.6 %all_to_all.15.n_ref = bf16[8,560,128]{2,1,0:T(8,128)(2,1)} all-to-all(bf16[8,560,128]{2,1,0:T(8,128)(2,1)S(1)} %head_rows.1), channel_id=1, replica_groups=mesh['seq'=8,'clip'=16] {'seq'}, dimensions={0} | all-to-all | bytes 2293760 | tf_op jit(solution)/shard_map/all_to_all | solution.py:556
  59.6 14.0 %attention.1 = (bf16[128,3072]{1,0:T(8,128)(2,1)}, bf16[128,3072]{1,0:T(8,128)(2,1)}) custom-call(s32[1,2]{1,0:T(1,128)} %flow_ref.5, bf16[8,560,128]{2,1,0:T(8,128)(2,1)} %all_to_all.15.n_ref, f32[72,128]{1,0:T(8,128)} %gram.1.gram_ref), custom_call_target="tpu_custom_call" | custom-call | tf_op jit(solution)/shard_map/attention/pallas_call | solution.py:558
Async XLA Ops:
  4.0 15.7 %all-to-all-start = ((bf16[16,8,640]{2,1,0:T(8,128)(2,1)}), bf16[16,8,640]{2,1,0:T(8,128)(2,1)S(1)}, u32[]{:S(2)}, u32[]{:S(2)}) async-start(bf16[16,8,640]{2,1,0:T(8,128)(2,1)} %bitcast.19), calls=%async_computation | async-start | bytes 327680 | tf_op jit(solution)/shard_map/all_to_all | solution.py:487
  19.8 0.7 copy-start.1
  24.0 13.4 %all-to-all-start.1 = ((bf16[16,8,1152]{2,1,0:T(8,128)(2,1)}), bf16[16,8,1152]{2,1,0:T(8,128)(2,1)S(1)}, u32[]{:S(2)}, u32[]{:S(2)}) async-start(bf16[16,8,1152]{2,1,0:T(8,128)(2,1)} %bitcast.18), calls=%async_computation.1 | async-start | bytes 589824 | tf_op jit(solution)/shard_map/all_to_all | solution.py:529
  27.6 9.9 %copy-start = (bf16[192,128]{1,0:T(8,128)(2,1)S(1)}, bf16[192,128]{1,0:T(8,128)(2,1)}, u32[]{:S(2)}) copy-start(bf16[192,128]{1,0:T(8,128)(2,1)} %conv.1.conv_ref) | copy-start | bytes 147460
where the time goes:
time: 74.1 us; the launch traced here: 73.7 us
  Pallas kernels  28.8 us (39%)
  blocking collectives  21.6 us (29%)
  waiting for transfers between devices  11.2 us (15%)
  starting transfers between devices  10.7 us (14%)
    all_to_all x1, blocking collectives, local(): every = lax.all_to_all(folded, 'seq', 0, 0, tiled=True)  21.6 us
    pallas_call x1, Pallas kernels, local(): pl.pallas_call(attention_kernel, grid=(1,), out_shape=[shape((128, peers...  14 us
    all_to_all x1, starting transfers between devices, local(): lax.all_to_all(partial.reshape(clips, 8, -1), 'clip', 0, 0, tiled=True)  7.13 us
    all_to_all x1, waiting for transfers between devices, local(): lax.all_to_all(partial.reshape(clips, 8, -1), 'clip', 0, 0, tiled=True)  5.75 us
    all_to_all x1, waiting for transfers between devices, local(): lax.all_to_all(second.reshape(clips, 8, -1), 'clip', 0, 0, tiled=True)  5.47 us
    pallas_call x1, Pallas kernels, local(): pl.pallas_call(gram_kernel, grid=(1,), out_shape=shape((72, 128), F32), i...  4.38 us
    pallas_call x1, Pallas kernels, local(): pl.pallas_call(time_kernel, grid=(1,), out_shape=shape((rows, 3 * width),...  3.58 us
    all_to_all x1, starting transfers between devices, local(): lax.all_to_all(second.reshape(clips, 8, -1), 'clip', 0, 0, tiled=True)  3.55 us
  transfers between devices with their start and end apart: 2, of which 2 were waited for; matrix products, arithmetic and copies ran while one was open for 0% of the time, Pallas kernels for 10%

commit v1 on v0

--- a/solution.py
+++ b/solution.py
@@ -523,7 +523,7 @@
             pltpu.VMEM((3, depth, width), BF),
             pltpu.SemaphoreType.DMA((6,)),
         ],
-        compiler_params=params(62),
+        compiler_params=params(60),
         name="time_rows",
     )(got, time_weight, gain, weight)
     got = lax.all_to_all(second.reshape(clips, 8, -1), "clip", 0, 0, tiled=True).reshape(rows, -1)

time: 74.1 us -> 74.1 us (level)
  no operation moved by 1% of the time
where the time goes in v1:
time: 74.1 us; the launch traced here: 73.7 us
  Pallas kernels  28.8 us (39%)
  blocking collectives  21.6 us (29%)
  waiting for transfers between devices  11.2 us (15%)
  starting transfers between devices  10.7 us (14%)
    all_to_all x1, blocking collectives, local(): every = lax.all_to_all(folded, 'seq', 0, 0, tiled=True)  21.6 us
    pallas_call x1, Pallas kernels, local(): pl.pallas_call(attention_kernel, grid=(1,), out_shape=[shape((128, peers...  14 us
    all_to_all x1, starting transfers between devices, local(): lax.all_to_all(partial.reshape(clips, 8, -1), 'clip', 0, 0, tiled=True)  7.13 us
    all_to_all x1, waiting for transfers between devices, local(): lax.all_to_all(partial.reshape(clips, 8, -1), 'clip', 0, 0, tiled=True)  5.75 us
    all_to_all x1, waiting for transfers between devices, local(): lax.all_to_all(second.reshape(clips, 8, -1), 'clip', 0, 0, tiled=True)  5.47 us
    pallas_call x1, Pallas kernels, local(): pl.pallas_call(gram_kernel, grid=(1,), out_shape=shape((72, 128), F32), i...  4.38 us
    pallas_call x1, Pallas kernels, local(): pl.pallas_call(time_kernel, grid=(1,), out_shape=shape((rows, 3 * width),...  3.58 us
    all_to_all x1, starting transfers between devices, local(): lax.all_to_all(second.reshape(clips, 8, -1), 'clip', 0, 0, tiled=True)  3.55 us
  transfers between devices with their start and end apart: 2, of which 2 were waited for; matrix products, arithmetic and copies ran while one was open for 0% of the time, Pallas kernels for 10%

profile of v1, /device:TPU:0, one launch (start us, length us, event | category | flops | bytes accessed | tf_op | source)
XLA Modules:
  0.0 73.7 jit_solution(12456729029672112650)
XLA Ops:
  0.6 3.4 %fold.1.after_ref = bf16[128,640]{1,0:T(8,128)(2,1)} custom-call(s32[1,2]{1,0:T(1,128)} %flow_ref.5, bf16[64,5120]{1,0:T(8,128)(2,1)} %embed_hbm.1, f32[1,5120]{1,0:T(1,128)} %bitcast.23, bf16[3,320,384]{2,1,0:T(8,128)(2,1)} %bitcast.16), custom_call_target="tpu_custom_call" | custom-call | tf_op jit(solution)/shard_map/fold/pallas_call | solution.py:472
  4.0 7.1 %all-to-all-start = ((bf16[16,8,640]{2,1,0:T(8,128)(2,1)}), bf16[16,8,640]{2,1,0:T(8,128)(2,1)S(1)}, u32[]{:S(2)}, u32[]{:S(2)}) async-start(bf16[16,8,640]{2,1,0:T(8,128)(2,1)} %bitcast.19), calls=%async_computation | async-start | bytes 327680 | tf_op jit(solution)/shard_map/all_to_all | solution.py:487
  11.2 2.8 %conv.1.conv_ref = bf16[192,128]{1,0:T(8,128)(2,1)} custom-call(bf16[4,128,384]{2,1,0:T(8,128)(2,1)} %bitcast.21, bf16[432,384]{1,0:T(8,128)(2,1)} %bitcast.22, f32[4,2,16,64]{3,2,1,0:T(8,128)} %bitcast.25, bf16[128,640]{1,0:T(8,128)(2,1)} %fold.1.after_ref), custom_call_target="tpu_custom_call" | custom-call | tf_op jit(solution)/shard_map/conv/pallas_call | solution.py:489
  14.0 5.8 %all-to-all-done = bf16[16,8,640]{2,1,0:T(8,128)(2,1)S(1)} async-done(((bf16[16,8,640]{2,1,0:T(8,128)(2,1)}), bf16[16,8,640]{2,1,0:T(8,128)(2,1)S(1)}, u32[]{:S(2)}, u32[]{:S(2)}) %all-to-all-start) | async-done | bytes 163872 | tf_op jit(solution)/shard_map/all_to_all | solution.py:487
  19.8 0.0 copy-start.1
  19.8 0.7 copy-done.1
  20.4 3.6 %time_rows.1.after_ref = bf16[128,1152]{1,0:T(8,128)(2,1)} custom-call(bf16[128,640]{1,0:T(8,128)(2,1)} %bitcast.20, bf16[256,5120]{1,0:T(8,128)(2,1)} %time_hbm.1, f32[1,5120]{1,0:T(1,128)} %bitcast.24, bf16[3,320,384]{2,1,0:T(8,128)(2,1)} %bitcast.17), custom_call_target="tpu_custom_call" | custom-call | tf_op jit(solution)/shard_map/time_rows/pallas_call | solution.py:513
  24.0 3.5 %all-to-all-start.1 = ((bf16[16,8,1152]{2,1,0:T(8,128)(2,1)}), bf16[16,8,1152]{2,1,0:T(8,128)(2,1)S(1)}, u32[]{:S(2)}, u32[]{:S(2)}) async-start(bf16[16,8,1152]{2,1,0:T(8,128)(2,1)} %bitcast.18), calls=%async_computation.1 | async-start | bytes 589824 | tf_op jit(solution)/shard_map/all_to_all | solution.py:529
  27.6 0.0 copy-start
  27.6 4.4 %gram.1.gram_ref = f32[72,128]{1,0:T(8,128)} custom-call(s32[1,2]{1,0:T(1,128)} %flow_ref.5, bf16[64,5120]{1,0:T(8,128)(2,1)} %embed_hbm.1, bf16[256,5120]{1,0:T(8,128)(2,1)} %time_hbm.1, bf16[128,1152]{1,0:T(8,128)(2,1)} %time_rows.1.after_ref), custom_call_target="tpu_custom_call" | custom-call | tf_op jit(solution)/shard_map/gram/pallas_call | solution.py:531
  32.0 5.5 %all-to-all-done.1 = bf16[16,8,1152]{2,1,0:T(8,128)(2,1)S(1)} async-done(((bf16[16,8,1152]{2,1,0:T(8,128)(2,1)}), bf16[16,8,1152]{2,1,0:T(8,128)(2,1)S(1)}, u32[]{:S(2)}, u32[]{:S(2)}) %all-to-all-start.1) | async-done | bytes 294944 | tf_op jit(solution)/shard_map/all_to_all | solution.py:529
  37.4 0.0 copy-done
  37.4 0.6 head_rows.1
  38.1 21.6 %all_to_all.15.n_ref = bf16[8,560,128]{2,1,0:T(8,128)(2,1)} all-to-all(bf16[8,560,128]{2,1,0:T(8,128)(2,1)S(1)} %head_rows.1), channel_id=1, replica_groups=mesh['seq'=8,'clip'=16] {'seq'}, dimensions={0} | all-to-all | bytes 2293760 | tf_op jit(solution)/shard_map/all_to_all | solution.py:556
  59.6 14.0 %attention.1 = (bf16[128,3072]{1,0:T(8,128)(2,1)}, bf16[128,3072]{1,0:T(8,128)(2,1)}) custom-call(s32[1,2]{1,0:T(1,128)} %flow_ref.5, bf16[8,560,128]{2,1,0:T(8,128)(2,1)} %all_to_all.15.n_ref, f32[72,128]{1,0:T(8,128)} %gram.1.gram_ref), custom_call_target="tpu_custom_call" | custom-call | tf_op jit(solution)/shard_map/attention/pallas_call | solution.py:558
Async XLA Ops:
  4.0 15.7 %all-to-all-start = ((bf16[16,8,640]{2,1,0:T(8,128)(2,1)}), bf16[16,8,640]{2,1,0:T(8,128)(2,1)S(1)}, u32[]{:S(2)}, u32[]{:S(2)}) async-start(bf16[16,8,640]{2,1,0:T(8,128)(2,1)} %bitcast.19), calls=%async_computation | async-start | bytes 327680 | tf_op jit(solution)/shard_map/all_to_all | solution.py:487
  19.8 0.7 copy-start.1
  24.0 13.4 %all-to-all-start.1 = ((bf16[16,8,1152]{2,1,0:T(8,128)(2,1)}), bf16[16,8,1152]{2,1,0:T(8,128)(2,1)S(1)}, u32[]{:S(2)}, u32[]{:S(2)}) async-start(bf16[16,8,1152]{2,1,0:T(8,128)(2,1)} %bitcast.18), calls=%async_computation.1 | async-start | bytes 589824 | tf_op jit(solution)/shard_map/all_to_all | solution.py:529
  27.6 9.9 %copy-start = (bf16[192,128]{1,0:T(8,128)(2,1)S(1)}, bf16[192,128]{1,0:T(8,128)(2,1)}, u32[]{:S(2)}) copy-start(bf16[192,128]{1,0:T(8,128)(2,1)} %conv.1.conv_ref) | copy-start | bytes 147460
